TPU v7x, 256 devices: a whole 4x4x8 slice. The times are simulated.
256 devices in a mesh: range: 4 (over x), depth: 64 (over y, z, core).
Axes of the slice: x: 4, y: 4, z: 8, core: 2. Of those that a mesh axis runs over, the one named last changes fastest.
Arguments:
- transfer_down: bfloat16 [2, 2, 4096, 4096], P(None, None, 'depth'), may hold values from -0.0625 to 0.0625
- transfer_up: bfloat16 [2, 2, 4096, 4096], P(None, None, 'depth'), may hold values from -0.0625 to 0.0625
- field_from_top: bfloat16 [2, 2, 4096, 4096], P(None, None, 'depth'), may hold values from -0.0625 to 0.0625
- field_from_bottom: bfloat16 [2, 2, 4096, 4096], P(None, None, 'depth'), may hold values from -0.0625 to 0.0625
- source_to_bottom: bfloat16 [2, 2, 4096, 4096], P(None, None, 'depth'), may hold values from -6 to 6
- source_to_top: bfloat16 [2, 2, 4096, 4096], P(None, None, 'depth'), may hold values from -6 to 6
- profile: int32 [4], P('range'), may hold values from 0 to 1
- source_depth: int32 [256], replicated, may hold values from 0 to 4095
Outputs:
- down_traces: bfloat16 [4, 2, 4096, 256], P('range', None, 'depth')
- up_traces: bfloat16 [4, 2, 4096, 256], P('range', None, 'depth')
- midline_field: float32 [4, 2, 4096, 256], P('range', None, 'depth')
All inputs are finite; a program needn't handle non-finite values.
Results may differ from a plain program's by a relative error of at most 0.0033.
Values may be sent and summed in bfloat16 or wider, within the bound.
A program may use at most 128 MiB of HBM per device.

v0:
```python
import jax
import jax.numpy as jnp
from jax import lax
from jax.sharding import PartitionSpec as P


def from_behind(block, axis, distance):
    devices = range(lax.axis_size(axis))
    route = [(i - distance, i) for i in devices if i - distance in devices]
    return lax.ppermute(block, axis, route)


def complex_apply(matrix, segment):
    real_part = jnp.dot(matrix[0], segment[0], preferred_element_type=jnp.float32) - jnp.dot(
        matrix[1], segment[1], preferred_element_type=jnp.float32
    )
    imag_part = jnp.dot(matrix[0], segment[1], preferred_element_type=jnp.float32) + jnp.dot(
        matrix[1], segment[0], preferred_element_type=jnp.float32
    )
    return jnp.stack([real_part, imag_part])


def select_profile(matrix, profile_index):
    return lax.dynamic_index_in_dim(matrix, profile_index, 0, keepdims=False)


def pass_trace(trace, direction):
    if direction > 0:
        return from_behind(trace, "range", 1)
    return from_behind(trace, "range", -1)


def apply_gathered(incoming, matrices, direction):

    def accumulate(segment):
        return tuple((complex_apply(matrix, segment) for matrix in matrices))

    if direction > 0:
        return accumulate(lax.all_gather(incoming, "depth", axis=1, tiled=True))
    return accumulate(lax.all_gather(incoming, "depth", axis=1, tiled=True))


def recurrent_sweep(force, transfer, recon, direction, layers):
    current = force
    for sweep_step in range(layers - 1):
        incoming = pass_trace(current, direction)
        matrices = (transfer, recon) if sweep_step == layers - 2 else (transfer,)
        results = apply_gathered(incoming, matrices, direction)
        current = (force.astype(jnp.float32) + results[0]).astype(jnp.bfloat16)
    return (current, results[1])


def body(
    transfer_down,
    transfer_up,
    field_from_top,
    field_from_bottom,
    source_to_bottom,
    source_to_top,
    profile,
    source_depth,
):
    layer_index = lax.axis_index("range")
    layers = lax.axis_size("range")
    profile_index = profile[0]
    down_matrix = select_profile(transfer_down, profile_index)
    up_matrix = select_profile(transfer_up, profile_index)
    top_recon = select_profile(field_from_top, profile_index)
    bottom_recon = select_profile(field_from_bottom, profile_index)
    sources = source_depth.shape[0]
    active = (jnp.arange(sources) % layers == layer_index)[None, None, :]
    nothing = jnp.zeros((), jnp.bfloat16)
    force_down = jnp.where(
        active,
        jnp.take(select_profile(source_to_bottom, profile_index), source_depth, axis=2),
        nothing,
    )
    force_up = jnp.where(
        active,
        jnp.take(select_profile(source_to_top, profile_index), source_depth, axis=2),
        nothing,
    )
    down_traces, top_part = recurrent_sweep(force_down, down_matrix, top_recon, 1, layers)
    up_traces, bottom_part = recurrent_sweep(force_up, up_matrix, bottom_recon, -1, layers)
    midline = top_part + bottom_part
    return (down_traces[None], up_traces[None], midline[None])


def solution(mesh):
    placed = (
        P(None, None, "depth", None),
        P(None, None, "depth", None),
        P(None, None, "depth", None),
        P(None, None, "depth", None),
        P(None, None, "depth", None),
        P(None, None, "depth", None),
        P("range"),
        P(),
    )
    return jax.shard_map(
        body,
        mesh=mesh,
        in_specs=placed,
        out_specs=(
            P("range", None, "depth", None),
            P("range", None, "depth", None),
            P("range", None, "depth", None),
        ),
        check_vma=False,
    )
```

profile of v0, /device:TPU:1, one launch (start us, length us, event | category | flops | bytes accessed | tf_op | source)
XLA Modules:
  0.0 536.5 jit_solution(18344297819079802744)
XLA Ops:
  8.0 0.7 compare_select_fusion
  8.7 0.7 compare_and_fusion
  9.4 2.7 constant_dynamic-slice_fusion
  12.1 5.5 %copy.13 = bf16[1,2,64,4096]{2,1,3,0:T(2,128)(2,1)} copy(bf16[1,2,64,4096]{3,2,1,0:T(8,128)(2,1)} %get-tuple-element.8) | data formatting | bytes 2097152 | tf_op jit(solution)/shard_map/jit(dynamic_index_in_dim)/dynamic_slice | solution.py:24
  17.7 2.5 gather_fusion.1
  20.3 3.9 copy.11
  24.2 2.5 gather_fusion
  26.9 1.3 collective-permute-start.3
  28.2 4.3 collective-permute-done.3
  32.5 0.6 copy-done.5
  33.2 3.4 collective-permute-start
  36.6 1.3 collective-permute-done
  38.6 78.6 %all-gather.13.cloned.1.call-done = bf16[2,4096,256]{2,1,0:T(8,128)(2,1)} async-done(((bf16[2,64,256]{2,1,0:T(8,128)(2,1)}), bf16[2,4096,256]{2,1,0:T(8,128)(2,1)}) %all-gather.13.cloned.1.call-update) | async-done | bytes 4194320 | tf_op jit(solution)/shard_map/all_gather | solution.py:40
  117.2 2.2 fusion.8
  119.4 2.1 fusion.53
  122.5 1.3 collective-permute-start.4
  123.8 3.7 collective-permute-done.4
  128.2 68.8 %all-gather.7.cloned.1.call-done = bf16[2,4096,256]{2,1,0:T(8,128)(2,1)} async-done(((bf16[2,64,256]{2,1,0:T(8,128)(2,1)}), bf16[2,4096,256]{2,1,0:T(8,128)(2,1)}) %all-gather.7.cloned.1.call-update) | async-done | bytes 4194320 | tf_op jit(solution)/shard_map/all_gather | solution.py:39
  197.0 2.4 fusion
  199.4 2.2 fusion.61
  201.6 1.5 fusion.3
  203.1 1.5 fusion.63
  204.7 3.1 collective-permute-start.1
  207.8 1.3 collective-permute-done.1
  209.8 67.0 %all-gather.15.cloned.1.call-done = bf16[2,4096,256]{2,1,0:T(8,128)(2,1)} async-done(((bf16[2,64,256]{2,1,0:T(8,128)(2,1)}), bf16[2,4096,256]{2,1,0:T(8,128)(2,1)}) %all-gather.15.cloned.1.call-update) | async-done | bytes 4194320 | tf_op jit(solution)/shard_map/all_gather | solution.py:40
  276.7 2.2 fusion.12
  278.9 2.1 fusion.49
  282.0 1.3 collective-permute-start.5
  283.3 3.7 collective-permute-done.5
  287.7 68.6 %all-gather.9.cloned.1.call-done = bf16[2,4096,256]{2,1,0:T(8,128)(2,1)} async-done(((bf16[2,64,256]{2,1,0:T(8,128)(2,1)}), bf16[2,4096,256]{2,1,0:T(8,128)(2,1)}) %all-gather.9.cloned.1.call-update) | async-done | bytes 4194320 | tf_op jit(solution)/shard_map/all_gather | solution.py:39
  356.3 2.4 fusion.4
  358.7 2.2 fusion.57
  360.9 1.5 fusion.7
  362.4 1.5 fusion.59
  364.0 3.3 collective-permute-start.2
  367.3 1.1 collective-permute-done.2
  369.1 66.9 %all-gather.17.cloned.1.call-done = bf16[2,4096,256]{2,1,0:T(8,128)(2,1)} async-done(((bf16[2,64,256]{2,1,0:T(8,128)(2,1)}), bf16[2,4096,256]{2,1,0:T(8,128)(2,1)}) %all-gather.17.cloned.1.call-update) | async-done | bytes 4194320 | tf_op jit(solution)/shard_map/all_gather | solution.py:40
  435.9 2.2 fusion.26
  438.1 2.1 fusion.33
  441.2 0.6 fusion.70
  441.8 73.7 %all-gather.11.cloned.1.call-done = bf16[2,4096,256]{2,1,0:T(8,128)(2,1)} async-done(((bf16[2,64,256]{2,1,0:T(8,128)(2,1)}), bf16[2,4096,256]{2,1,0:T(8,128)(2,1)}) %all-gather.11.cloned.1.call-update) | async-done | bytes 4194320 | tf_op jit(solution)/shard_map/all_gather | solution.py:39
  515.5 2.4 fusion.18
  517.9 2.4 fusion.23
  520.3 1.7 fusion.41
  522.0 1.5 fusion.45
  523.5 0.6 fusion.71
  525.1 1.1 copy-done.15
  529.0 0.7 maximum_add_fusion
  (64 shorter events, 10.3 us)
Async XLA Ops:
  7.2 110.0 %copy-start = (bf16[2,2,64,4096]{3,2,1,0:T(8,128)(2,1)S(1)}, bf16[2,2,64,4096]{3,2,1,0:T(8,128)(2,1)}, u32[]{:S(2)}) copy-start(bf16[2,2,64,4096]{3,2,1,0:T(8,128)(2,1)} %param.11) | copy-start | bytes 6291460
  7.2 110.0 %all-gather.13.cloned.1.call-start = ((), (), s32[]{:S(2)}) async-start(), calls=%async_computation.3 | async-start | bytes 4259840 | tf_op jit(solution)/shard_map/all_gather | solution.py:40
  26.9 5.6 %collective-permute-start.3 = (bf16[2,64,256]{2,1,0:T(8,128)(2,1)S(1)}, bf16[2,64,256]{2,1,0:T(8,128)(2,1)S(1)}, u32[]{:S(2)}, u32[]{:S(2)}) collective-permute-start(bf16[2,64,256]{2,1,0:T(8,128)(2,1)S(1)} %get-tuple-element.4), channel_id=1, source_target_pairs={{64,0},{128,64},{192,128},{65,1},{129,65},{193,129},{66,2},{130,66... | collective-permute-start | bytes 196616 | tf_op jit(solution)/shard_map/ppermute | solution.py:10
  32.5 0.6 copy-start.5
  33.1 163.8 %all-gather.7.cloned.1.call-start = ((), (), s32[]{:S(2)}) async-start(), calls=%async_computation | async-start | bytes 4259840 | tf_op jit(solution)/shard_map/all_gather | solution.py:39
  33.2 4.7 collective-permute-start
  37.9 0.6 copy-start.1
  38.5 238.2 %all-gather.15.cloned.1.call-start = ((), (), s32[]{:S(2)}) async-start(), calls=%async_computation.4 | async-start | bytes 4259840 | tf_op jit(solution)/shard_map/all_gather | solution.py:40
  117.2 4.3 copy-start.13
  122.5 5.0 collective-permute-start.4
  127.5 0.6 copy-start.2
  128.1 228.2 %all-gather.9.cloned.1.call-start = ((), (), s32[]{:S(2)}) async-start(), calls=%async_computation.1 | async-start | bytes 4259840 | tf_op jit(solution)/shard_map/all_gather | solution.py:39
  197.0 4.6 copy-start.9
  204.7 4.4 collective-permute-start.1
  209.1 0.6 copy-start.3
  209.7 226.2 %all-gather.17.cloned.1.call-start = ((), (), s32[]{:S(2)}) async-start(), calls=%async_computation.5 | async-start | bytes 4259840 | tf_op jit(solution)/shard_map/all_gather | solution.py:40
  276.7 4.3 copy-start.10
  282.0 5.0 collective-permute-start.5
  287.0 0.6 copy-start.4
  287.6 227.9 %all-gather.11.cloned.1.call-start = ((), (), s32[]{:S(2)}) async-start(), calls=%async_computation.2 | async-start | bytes 4259840 | tf_op jit(solution)/shard_map/all_gather | solution.py:39
  356.3 4.6 copy-start.11
  364.0 4.4 collective-permute-start.2
  368.4 0.6 copy-start.6
  435.9 4.3 copy-start.7
  515.5 4.8 copy-start.12
  517.9 6.2 %copy-start.14 = (bf16[2,2,64,4096]{3,2,1,0:T(8,128)(2,1)S(1)}, bf16[2,2,64,4096]{3,2,1,0:T(8,128)(2,1)}, u32[]{:S(2)}) copy-start(bf16[2,2,64,4096]{3,2,1,0:T(8,128)(2,1)} %param.13) | copy-start | bytes 6291460
  520.3 3.8 copy-start.8
  524.6 1.6 copy-start.15
Sparse Core Ops, SparseCore 0:
  33.3 83.9 all-gather.12
  120.6 76.3 all-gather.6
  200.4 76.3 all-gather.14
  280.0 76.3 all-gather.8
  359.5 76.3 all-gather.16
  439.2 76.3 all-gather.10
where the time goes:
time: 537 us
  waiting for transfers between devices  439 us (82%)
  matrix products  42.4 us (8%)
  local copies, waits for them, and re-layouts  22.4 us (4%)
  between operations  15.3 us (3%)
  starting transfers between devices  13.9 us (3%)
    all_gather x6, waiting for transfers between devices, apply_gathered(): return accumulate(lax.all_gather(incoming, 'depth', axis=1, tiled=True))  424 us
    ppermute x6, waiting for transfers between devices, from_behind(): return lax.ppermute(block, axis, route)  15.5 us
    dot_general x8, matrix products, complex_apply(): jnp.dot(matrix[1], segment[0], preferred_element_type=jnp.float32)  14.6 us
    ppermute x6, starting transfers between devices, from_behind(): return lax.ppermute(block, axis, route)  13.6 us
    dot_general x8, matrix products, complex_apply(): jnp.dot(matrix[0], segment[1], preferred_element_type=jnp.float32)  13.2 us
    dynamic_slice x3, local copies, waits for them, and re-layouts, select_profile(): return lax.dynamic_index_in_dim(matrix, profile_index, 0, keepdims=False)  12.2 us
  transfers between devices with their start and end apart: 12, of which 12 were waited for; matrix products, arithmetic and copies ran while one was open for 6% of the time, Pallas kernels for 0%

commit v1 on v0

v1 whole, which is shorter than its diff:
```python
import functools

import jax
import jax.numpy as jnp
from jax import lax
from jax.experimental import pallas as pl
from jax.experimental.pallas import tpu as pltpu
from jax.sharding import PartitionSpec as P

MESH = pl.DeviceIdType.MESH
Y, Z, CORES = 4, 8, 2
PART = 32
DZ = (4, 3, -3, 2, -2, 1, -1)
DY = (2, 1, -1)
NEAR_Z = (5, 6, 3, 4, 1, 2, 0)
NEAR_Y = (1, 2, 0)
BF16, F32 = jnp.bfloat16, jnp.float32


def wait_bytes(ref, sem):
    pltpu.make_async_copy(ref, ref, sem).wait()


def rotate_parts(product):
    rows, columns = product.shape[0] // 2, product.shape[1]
    swapped = pltpu.roll(product[rows:], columns // 2, 1)
    lane = lax.broadcasted_iota(jnp.int32, swapped.shape, 1)
    return product[:rows] + jnp.where(lane < columns // 2, -swapped, swapped)


def kernel(
    profile, depth, t_down, t_up, f_top, f_bottom, s_bottom, s_top,
    down_out, up_out, mid_out,
    mats, srcs, seg, traces, fields, forces, my_trace, my_field, place, prof_v, prof_s,
    mat_sem, src_sem, z_sem, y_sem, b_sem, a_sem, sib_sem,
    w1_send, b_send, a_send, sib_send, tr_send, tr_recv, mid_send, mid_recv, p_send, p_recv, p_local,
):
    layers = 4
    r = lax.axis_index("range")
    d = lax.axis_index("depth")
    y, z, c = d // (Z * CORES), (d // CORES) % Z, d % CORES

    def at(yy, zz, cc):
        return (r, ((yy % Y) * Z + zz % Z) * CORES + cc)

    sibling = at(y, z, 1 - c)

    barrier = pltpu.get_barrier_semaphore()
    peers = [at(y, z + k, c) for k in range(1, Z)] + [at(y + k, z, c) for k in range(1, Y)] + [sibling]
    peers += [((r + k) % layers, d) for k in range(1, layers)]
    for peer in peers:
        pl.semaphore_signal(barrier, inc=1, device_id=peer, device_id_type=MESH)

    src_copies = [
        pltpu.make_async_copy(ref, srcs.at[i], src_sem.at[i]) for i, ref in enumerate((s_bottom, s_top))
    ]
    mat_copies = [
        pltpu.make_async_copy(ref, mats.at[i // 2, i % 2], mat_sem.at[i])
        for i, ref in enumerate((t_down, f_top, t_up, f_bottom))
    ]
    for copy in src_copies + mat_copies:
        copy.start()

    my_profile = profile[0]
    prof_v[r] = jnp.full(prof_v.shape[1:], my_profile, jnp.int32)

    every = depth[...]
    pick_s = lax.broadcasted_iota(jnp.int32, (256, 128), 0)
    pick_j = lax.broadcasted_iota(jnp.int32, (256, 128), 1)
    pick = jnp.where(pick_s == 4 * (pick_j % 64) + r, 1.0, 0.0).astype(BF16)
    high = jnp.broadcast_to(every // 64, (16, 256)).astype(F32).astype(BF16)
    low = jnp.broadcast_to(every % 64, (16, 256)).astype(F32).astype(BF16)
    chosen = jnp.dot(high, pick, preferred_element_type=F32) * 64.0 + jnp.dot(low, pick, preferred_element_type=F32)
    chosen = chosen[0:1].astype(jnp.int32)

    for copy in src_copies:
        copy.wait()
    lane = lax.broadcasted_iota(jnp.int32, (64, 128), 1)
    total = jnp.zeros((256, 128), F32)
    step = 1024
    for k0 in range(0, 4096, step):
        rows = lax.broadcasted_iota(jnp.int32, (step, 128), 0) + k0
        hot = jnp.where(rows == chosen, 1.0, 0.0).astype(BF16)
        left = srcs[:, my_profile, :, :, pl.ds(k0, step)].reshape(256, step)
        total += jnp.dot(left, hot, preferred_element_type=F32)
    total = total.reshape(2, 2, 64, 128)
    for i in range(2):
        forces[i] = jnp.where(lane < 64, total[i, 0], total[i, 1]).astype(BF16)

    middle = jnp.logical_or(r == 1, r == 2)
    way_01 = jnp.where(r < 2, 0, 1)
    way_2 = jnp.where(r % 2 == 0, 0, 1)
    ways = (way_01, way_01, way_2)
    layer_of = (jnp.where(r % 2 == 0, 1, 2), jnp.where(r < 2, r + 2, r - 2), jnp.where(r % 2 == 0, 3, 0))

    pl.semaphore_wait(barrier, len(peers))

    profile_copies = [
        pltpu.make_async_remote_copy(
            src_ref=prof_v.at[r], dst_ref=prof_v.at[r], send_sem=p_send.at[k], recv_sem=p_recv.at[r],
            device_id=((r + k) % layers, d), device_id_type=MESH,
        )
        for k in range(1, layers)
    ]

    def block(k, yy, zz, low=0, count=64):
        return seg.at[k, (yy % Y) * Z + zz % Z, c, pl.ds(low, count)]

    def row(k, yy, core):
        return seg.at[k, pl.ds((yy % Y) * Z, Z), core]

    def put(ref, send, recv, to):
        pltpu.make_async_remote_copy(
            src_ref=ref, dst_ref=ref, send_sem=send, recv_sem=recv, device_id=to, device_id_type=MESH
        ).start()

    def send_own(k):
        own = block(k, y, z)
        for i, dz in enumerate(DZ):
            put(own, w1_send.at[k], z_sem.at[k, i], at(y, z + dz, c))
        for j, dy in enumerate(DY):
            put(own, w1_send.at[k], y_sem.at[k, j], at(y + dy, z, c))

    def pass_y(k, j):
        got = DY[j]
        wait_bytes(block(k, y - got, z), y_sem.at[k, j])
        for dz in DZ:
            put(block(k, y - got, z, 0, PART), a_send.at[k], a_sem.at[k, j], at(y, z + dz, c))

    def pass_z(k, i):
        got = DZ[i]
        wait_bytes(block(k, y, z - got), z_sem.at[k, i])
        for j, dy in enumerate(DY):
            put(block(k, y, z - got, PART, 64 - PART), b_send.at[k], b_sem.at[k, j], at(y + dy, z, c))

    def multiply(k, kind, yy, prof):
        left = mats[ways[k], kind, prof, :, :, pl.ds(pl.multiple_of(yy * 1024, 1024), 1024)]
        right = seg[k, pl.ds(yy * Z, Z)].reshape(1024, 128)
        return jnp.dot(left.reshape(128, 1024), right, preferred_element_type=F32)

    def collect(k, prof):
        pass_y(k, 1)
        pass_y(k, 2)
        pass_z(k, 5)
        pass_z(k, 6)
        pass_y(k, 0)
        for i in (3, 4, 1, 2, 0):
            pass_z(k, i)
        put(row(k, y, c), sib_send.at[k], sib_sem.at[k, 3], sibling)
        for j in NEAR_Y:
            wait_bytes(seg.at[k, pl.ds(0, Z - 1), c, pl.ds(PART, 64 - PART)], b_sem.at[k, j])
            wait_bytes(seg.at[k, pl.ds(0, Z - 1), c, pl.ds(0, PART)], a_sem.at[k, j])
            put(row(k, y - DY[j], c), sib_send.at[k], sib_sem.at[k, j], sibling)
        total = jnp.zeros((128, 128), F32)
        for j in (3,) + NEAR_Y:
            yy = (y - (DY + (0,))[j]) % Y
            wait_bytes(row(k, yy, 1 - c), sib_sem.at[k, j])
            total += multiply(k, 0, yy, prof)
        return rotate_parts(total)

    def field(k, prof):
        total = jnp.zeros((128, 128), F32)
        for yy in range(Y):
            total += multiply(k, 1, yy, prof)
        return rotate_parts(total)

    def to_layer(k, mine, send, theirs, recv):
        return pltpu.make_async_remote_copy(
            src_ref=mine.at[k], dst_ref=theirs.at[r], send_sem=send.at[k], recv_sem=recv.at[r],
            device_id=(layer_of[k], d), device_id_type=MESH,
        )

    trace_copies = [to_layer(k, my_trace, tr_send, traces, tr_recv) for k in range(3)]
    field_copies = [to_layer(k, my_field, mid_send, fields, mid_recv) for k in range(3)]

    seg[0, y * Z + z, c] = forces[way_01]
    send_own(0)
    for copy in profile_copies:
        copy.start()

    i_in = lax.broadcasted_iota(jnp.int32, (512, 512), 0)
    i_out = lax.broadcasted_iota(jnp.int32, (512, 512), 1)
    goal = ((i_in % 128) // 64) * 256 + 4 * (i_in % 64) + i_in // 128
    place[...] = jnp.where(i_out == goal, 1.0, 0.0).astype(BF16)
    fields[r] = jnp.zeros((64, 128), F32)

    for copy in mat_copies:
        copy.wait()
    for k in range(1, layers):
        other = (r + k) % layers
        wait_bytes(prof_v.at[other], p_recv.at[other])
    to_scalar = pltpu.make_async_copy(prof_v, prof_s, p_local)
    for copy in profile_copies:
        copy.wait_send()
    to_scalar.start()
    to_scalar.wait()

    for k in range(3):
        prof = prof_s[layer_of[k], 0, 0]
        trace = collect(k, prof).astype(BF16)
        my_trace[k] = trace
        if k == 0:
            seg[1, y * Z + z, c] = trace
        elif k == 1:
            seg[2, y * Z + z, c] = jnp.where(middle, forces[1 - way_01], trace)
        if k < 2:
            send_own(k + 1)
        trace_copies[k].start()
        my_field[k] = field(k, prof)
        field_copies[k].start()

    for k in range(1, layers):
        other = (r + k) % layers
        wait_bytes(traces.at[other], tr_recv.at[other])
    traces[r] = forces[0]
    empty = jnp.zeros((64, 128), BF16)
    down = [jnp.where(i <= r, traces[i], empty) for i in range(layers)]
    traces[r] = forces[1]
    up = [jnp.where(i >= r, traces[i], empty) for i in range(layers)]
    both = jnp.concatenate([jnp.concatenate(down, axis=1), jnp.concatenate(up, axis=1)], axis=0)
    moved = jnp.dot(both, place[...], preferred_element_type=F32).astype(BF16)
    for part in range(2):
        down_out[0, part] = moved[:64, part * 256:(part + 1) * 256]
        up_out[0, part] = moved[64:, part * 256:(part + 1) * 256]

    for k in range(1, layers):
        other = (r + k) % layers
        wait_bytes(fields.at[other], mid_recv.at[other])
    whole = jnp.concatenate([fields[i] for i in range(layers)], axis=1)
    first = whole.astype(BF16)
    rest = whole - first.astype(F32)
    second = rest.astype(BF16)
    third = (rest - second.astype(F32)).astype(BF16)
    pieces = jnp.concatenate([first, second, third], axis=0)
    moved = jnp.dot(pieces, place[...], preferred_element_type=F32)
    moved = moved[0:64] + moved[64:128] + moved[128:192]
    for part in range(2):
        mid_out[0, part] = moved[:, part * 256:(part + 1) * 256]

    for k in range(3):
        wait_bytes(seg.at[k, pl.ds(0, 5)], w1_send.at[k])
        wait_bytes(seg.at[k, pl.ds(0, 21), 0, pl.ds(0, 64 - PART)], b_send.at[k])
        wait_bytes(seg.at[k, pl.ds(0, 21), 0, pl.ds(0, PART)], a_send.at[k])
        wait_bytes(seg.at[k, :, 0], sib_send.at[k])
        trace_copies[k].wait_send()
        field_copies[k].wait_send()


def body(
    transfer_down, transfer_up, field_from_top, field_from_bottom, source_to_bottom, source_to_top, profile, source_depth,
):
    hbm = pl.BlockSpec(memory_space=pl.ANY)
    vmem = pl.BlockSpec(memory_space=pltpu.VMEM)
    dma = pltpu.SemaphoreType.DMA
    return pl.pallas_call(
        kernel,
        out_shape=(
            jax.ShapeDtypeStruct((1, 2, 64, 256), BF16),
            jax.ShapeDtypeStruct((1, 2, 64, 256), BF16),
            jax.ShapeDtypeStruct((1, 2, 64, 256), F32),
        ),
        in_specs=[pl.BlockSpec(memory_space=pltpu.SMEM), vmem] + [hbm] * 6,
        out_specs=(vmem, vmem, vmem),
        scratch_shapes=[
            pltpu.VMEM((2, 2, 2, 2, 64, 4096), BF16),
            pltpu.VMEM((2, 2, 2, 64, 4096), BF16),
            pltpu.VMEM((3, Y * Z, CORES, 64, 128), BF16),
            pltpu.VMEM((4, 64, 128), BF16),
            pltpu.VMEM((4, 64, 128), F32),
            pltpu.VMEM((2, 64, 128), BF16),
            pltpu.VMEM((3, 64, 128), BF16),
            pltpu.VMEM((3, 64, 128), F32),
            pltpu.VMEM((512, 512), BF16),
            pltpu.VMEM((4, 8, 128), jnp.int32),
            pltpu.SMEM((4, 8, 128), jnp.int32),
            dma((4,)), dma((2,)),
            dma((3, 7)), dma((3, 3)), dma((3, 3)), dma((3, 3)), dma((3, 4)),
            dma((3,)), dma((3,)), dma((3,)), dma((3,)),
            dma((3,)), dma((4,)), dma((3,)), dma((4,)),
            dma((4,)), dma((4,)), dma(()),
        ],
        compiler_params=pltpu.CompilerParams(
            collective_id=0, has_side_effects=True, vmem_limit_bytes=60 * 2**20
        ),
        cost_estimate=pl.CostEstimate(flops=10**9, bytes_accessed=13 * 2**20, transcendentals=0),
        name="sweeps",
    )(
        profile, source_depth.reshape(1, 256),
        transfer_down, transfer_up, field_from_top, field_from_bottom, source_to_bottom, source_to_top,
    )


def solution(mesh):
    rows = P(None, None, "depth", None)
    return jax.shard_map(
        body,
        mesh=mesh,
        in_specs=(rows,) * 6 + (P("range"), P()),
        out_specs=(P("range", None, "depth", None),) * 3,
        check_vma=False,
    )
```

time: 537 us -> 60.5 us (0.11)
  waiting for transfers between devices: 439 us -> 0 us
  Pallas kernels: 0 us -> 54.5 us
  matrix products: 42.4 us -> 0 us
  local copies, waits for them, and re-layouts: 22.4 us -> 4.51 us
  between operations: 15.3 us -> 1.29 us
  starting transfers between devices: 13.9 us -> 0 us
    all_gather x6 -> x0, waiting for transfers between devices: 424 us -> none  [apply_gathered(): return accumulate(lax.all_gather(incoming, 'depth', axis=1, tiled=True))]
    pallas_call x0 -> x1, Pallas kernels: none -> 54.5 us  [body(): pl.pallas_call(kernel, out_shape=(jax.ShapeDtypeStruct((1, 2, 64, 256), B...]
    dot_general x32 -> x0, matrix products: 42.4 us -> none  [the longest x8 14.6 us: complex_apply(): jnp.dot(matrix[1], segment[0], preferred_element_type=jnp.float32)]
    ppermute x6 -> x0, waiting for transfers between devices: 15.5 us -> none  [from_behind(): return lax.ppermute(block, axis, route)]
    ppermute x6 -> x0, starting transfers between devices: 13.6 us -> none  [from_behind(): return lax.ppermute(block, axis, route)]
    dynamic_slice x3 -> x0, local copies, waits for them, and re-layouts: 12.2 us -> none  [select_profile(): return lax.dynamic_index_in_dim(matrix, profile_index, 0, keepdims=False)]
  transfers between devices with their start and end apart: 12 -> 0, of which waited for: 12 -> 0; matrix products, arithmetic and copies ran while one was open for 6% -> 0% of each run, Pallas kernels for 0% -> 0%
where the time goes in v1:
time: 60.5 us; the launch traced here: 60.3 us
  Pallas kernels  54.5 us (90%)
  local copies, waits for them, and re-layouts  4.51 us (7%)
  between operations  1.29 us (2%)
    pallas_call x1, Pallas kernels, body(): pl.pallas_call(kernel, out_shape=(jax.ShapeDtypeStruct((1, 2, 64, 256), B...  54.5 us
    unnamed x3, local copies, waits for them, and re-layouts  4.51 us

profile of v1, /device:TPU:1, one launch (start us, length us, event | category | flops | bytes accessed | tf_op | source)
XLA Modules:
  0.0 60.3 jit_solution(11083842045602183144)
XLA Ops:
  1.3 54.5 %sweeps.1 = (bf16[1,2,64,256]{3,2,1,0:T(8,128)(2,1)}, bf16[1,2,64,256]{3,2,1,0:T(8,128)(2,1)}, f32[1,2,64,256]{3,2,1,0:T(8,128)}) custom-call(s32[1]{0:T(128)S(6)} %copy.14.profile, s32[1,256]{1,0:T(1,128)} %bitcast.1, bf16[2,2,64,4096]{3,2,1,0:T(8,128)(2,1)} %t_down.1, bf16[2,2,64,4096]{3,2,1,0:T(8,128)(2,1)} %t_up.1, bf16[2,2,64,4096]{3,2,1,0:T(8,128)(2,1)} %f_top.1, ...), custom_call_target="tpu_custom_call" | custom-call | flops 1000000000 | bytes 13631488 | tf_op jit(solution)/shard_map/sweeps/pallas_call | solution.py:255
  55.8 1.5 %copy.15 = bf16[1,2,64,256]{3,2,1,0:T(8,128)(2,1)} copy(bf16[1,2,64,256]{3,2,1,0:T(8,128)(2,1)} %get-tuple-element.6) | data formatting | bytes 131072
  57.2 1.5 %copy.16 = bf16[1,2,64,256]{3,2,1,0:T(8,128)(2,1)} copy(bf16[1,2,64,256]{3,2,1,0:T(8,128)(2,1)} %get-tuple-element.7) | data formatting | bytes 131072
  58.7 1.6 %copy.17 = f32[1,2,64,256]{3,2,1,0:T(8,128)} copy(f32[1,2,64,256]{3,2,1,0:T(8,128)} %get-tuple-element.8) | data formatting | bytes 262144

commit v2 on v1

--- a/solution.py
+++ b/solution.py
@@ -9,11 +9,11 @@
 
 MESH = pl.DeviceIdType.MESH
 Y, Z, CORES = 4, 8, 2
-PART = 32
-DZ = (4, 3, -3, 2, -2, 1, -1)
-DY = (2, 1, -1)
-NEAR_Z = (5, 6, 3, 4, 1, 2, 0)
-NEAR_Y = (1, 2, 0)
+FAR_FIRST = [(dy, dz) for dy in (0, 1, -1, 2) for dz in (0, 1, -1, 2, -2, 3, -3, 4) if (dy, dz) != (0, 0)]
+FAR_FIRST.sort(key=lambda o: -abs(o[0]) - abs(o[1]))
+STRAIGHT = [o for o in FAR_FIRST if 0 in o]
+OFFSETS = sorted(FAR_FIRST, key=lambda o: abs(o[0]) + abs(o[1]) + (0 if 0 in o else 3.6))
+CHUNK, HALF = 1024, 2048
 BF16, F32 = jnp.bfloat16, jnp.float32
 
 
@@ -31,11 +31,11 @@
 def kernel(
     profile, depth, t_down, t_up, f_top, f_bottom, s_bottom, s_top,
     down_out, up_out, mid_out,
-    mats, srcs, seg, traces, fields, forces, my_trace, my_field, place, prof_v, prof_s,
-    mat_sem, src_sem, z_sem, y_sem, b_sem, a_sem, sib_sem,
-    w1_send, b_send, a_send, sib_send, tr_send, tr_recv, mid_send, mid_recv, p_send, p_recv, p_local,
+    mats, src_0, src_1, src_2, src_3, seg, traces, fields, forces, my_trace, my_field, place, prof_v, prof_s,
+    hot, mat_sem, src_sem, seg_send, seg_recv, sib_recv, tr_send, tr_recv, mid_send, mid_recv, p_send, p_recv, p_local,
 ):
     layers = 4
+    srcs = (src_0, src_1, src_2, src_3)
     r = lax.axis_index("range")
     d = lax.axis_index("depth")
     y, z, c = d // (Z * CORES), (d // CORES) % Z, d % CORES
@@ -51,15 +51,25 @@
     for peer in peers:
         pl.semaphore_signal(barrier, inc=1, device_id=peer, device_id_type=MESH)
 
+    down_first = r < 2
+    way_01 = jnp.where(down_first, 0, 1)
+
     src_copies = [
-        pltpu.make_async_copy(ref, srcs.at[i], src_sem.at[i]) for i, ref in enumerate((s_bottom, s_top))
+        [
+            pltpu.make_async_copy(ref.at[:, :, :, pl.ds(half * HALF, HALF)], srcs[2 * i + half], src_sem.at[i, half])
+            for i, ref in enumerate(refs) for half in range(2)
+        ]
+        for refs in ((s_bottom, s_top), (s_top, s_bottom))
     ]
+    for way in range(2):
+        @pl.when(way_01 == way)
+        def _():
+            for copy in src_copies[way]:
+                copy.start()
     mat_copies = [
         pltpu.make_async_copy(ref, mats.at[i // 2, i % 2], mat_sem.at[i])
         for i, ref in enumerate((t_down, f_top, t_up, f_bottom))
     ]
-    for copy in src_copies + mat_copies:
-        copy.start()
 
     my_profile = profile[0]
     prof_v[r] = jnp.full(prof_v.shape[1:], my_profile, jnp.int32)
@@ -73,27 +83,25 @@
     chosen = jnp.dot(high, pick, preferred_element_type=F32) * 64.0 + jnp.dot(low, pick, preferred_element_type=F32)
     chosen = chosen[0:1].astype(jnp.int32)
 
-    for copy in src_copies:
-        copy.wait()
+    for k0 in range(0, 4096, CHUNK):
+        rows = lax.broadcasted_iota(jnp.int32, (CHUNK, 128), 0) + k0
+        hot[pl.ds(k0, CHUNK)] = jnp.where(rows == chosen, 1.0, 0.0).astype(BF16)
     lane = lax.broadcasted_iota(jnp.int32, (64, 128), 1)
-    total = jnp.zeros((256, 128), F32)
-    step = 1024
-    for k0 in range(0, 4096, step):
-        rows = lax.broadcasted_iota(jnp.int32, (step, 128), 0) + k0
-        hot = jnp.where(rows == chosen, 1.0, 0.0).astype(BF16)
-        left = srcs[:, my_profile, :, :, pl.ds(k0, step)].reshape(256, step)
-        total += jnp.dot(left, hot, preferred_element_type=F32)
-    total = total.reshape(2, 2, 64, 128)
-    for i in range(2):
-        forces[i] = jnp.where(lane < 64, total[i, 0], total[i, 1]).astype(BF16)
+
+    def find_force(i):
+        total = jnp.zeros((128, 128), F32)
+        for half in range(2):
+            src = srcs[2 * i + half]
+            wait_bytes(src, src_sem.at[i, half])
+            total += jnp.dot(
+                src[my_profile].reshape(128, HALF), hot[pl.ds(half * HALF, HALF)], preferred_element_type=F32
+            )
+        return jnp.where(lane < 64, total[:64], total[64:]).astype(BF16)
 
     middle = jnp.logical_or(r == 1, r == 2)
-    way_01 = jnp.where(r < 2, 0, 1)
     way_2 = jnp.where(r % 2 == 0, 0, 1)
     ways = (way_01, way_01, way_2)
     layer_of = (jnp.where(r % 2 == 0, 1, 2), jnp.where(r < 2, r + 2, r - 2), jnp.where(r % 2 == 0, 3, 0))
-
-    pl.semaphore_wait(barrier, len(peers))
 
     profile_copies = [
         pltpu.make_async_remote_copy(
@@ -103,8 +111,8 @@
         for k in range(1, layers)
     ]
 
-    def block(k, yy, zz, low=0, count=64):
-        return seg.at[k, (yy % Y) * Z + zz % Z, c, pl.ds(low, count)]
+    def block(k, offset):
+        return seg.at[k, ((y - offset[0]) % Y) * Z + (z - offset[1]) % Z, c]
 
     def row(k, yy, core):
         return seg.at[k, pl.ds((yy % Y) * Z, Z), core]
@@ -114,24 +122,27 @@
             src_ref=ref, dst_ref=ref, send_sem=send, recv_sem=recv, device_id=to, device_id_type=MESH
         ).start()
 
+    def ship(k, held, offset):
+        put(
+            block(k, held), seg_send.at[k], seg_recv.at[k, (offset[0] % Y) * Z + offset[1] % Z],
+            at(y + offset[0] - held[0], z + offset[1] - held[1], c),
+        )
+
+    def to_sibling(k, held):
+        put(block(k, held), seg_send.at[k], sib_recv.at[k, held[0] % Y], sibling)
+
     def send_own(k):
-        own = block(k, y, z)
-        for i, dz in enumerate(DZ):
-            put(own, w1_send.at[k], z_sem.at[k, i], at(y, z + dz, c))
-        for j, dy in enumerate(DY):
-            put(own, w1_send.at[k], y_sem.at[k, j], at(y + dy, z, c))
-
-    def pass_y(k, j):
-        got = DY[j]
-        wait_bytes(block(k, y - got, z), y_sem.at[k, j])
-        for dz in DZ:
-            put(block(k, y - got, z, 0, PART), a_send.at[k], a_sem.at[k, j], at(y, z + dz, c))
-
-    def pass_z(k, i):
-        got = DZ[i]
-        wait_bytes(block(k, y, z - got), z_sem.at[k, i])
-        for j, dy in enumerate(DY):
-            put(block(k, y, z - got, PART, 64 - PART), b_send.at[k], b_sem.at[k, j], at(y + dy, z, c))
+        for offset in STRAIGHT:
+            ship(k, (0, 0), offset)
+        to_sibling(k, (0, 0))
+
+    def pass_on(k, held):
+        wait_bytes(block(k, held), seg_recv.at[k, (held[0] % Y) * Z + held[1] % Z])
+        for offset in FAR_FIRST:
+            if 0 not in offset:
+                if (offset[0], 0) == held if abs(offset[1]) <= 2 else (0, offset[1]) == held:
+                    ship(k, held, offset)
+        to_sibling(k, held)
 
     def multiply(k, kind, yy, prof):
         left = mats[ways[k], kind, prof, :, :, pl.ds(pl.multiple_of(yy * 1024, 1024), 1024)]
@@ -139,22 +150,12 @@
         return jnp.dot(left.reshape(128, 1024), right, preferred_element_type=F32)
 
     def collect(k, prof):
-        pass_y(k, 1)
-        pass_y(k, 2)
-        pass_z(k, 5)
-        pass_z(k, 6)
-        pass_y(k, 0)
-        for i in (3, 4, 1, 2, 0):
-            pass_z(k, i)
-        put(row(k, y, c), sib_send.at[k], sib_sem.at[k, 3], sibling)
-        for j in NEAR_Y:
-            wait_bytes(seg.at[k, pl.ds(0, Z - 1), c, pl.ds(PART, 64 - PART)], b_sem.at[k, j])
-            wait_bytes(seg.at[k, pl.ds(0, Z - 1), c, pl.ds(0, PART)], a_sem.at[k, j])
-            put(row(k, y - DY[j], c), sib_send.at[k], sib_sem.at[k, j], sibling)
+        for held in OFFSETS:
+            pass_on(k, held)
         total = jnp.zeros((128, 128), F32)
-        for j in (3,) + NEAR_Y:
-            yy = (y - (DY + (0,))[j]) % Y
-            wait_bytes(row(k, yy, 1 - c), sib_sem.at[k, j])
+        for dy in (0, 1, -1, 2):
+            yy = (y - dy) % Y
+            wait_bytes(row(k, yy, 1 - c), sib_recv.at[k, dy % Y])
             total += multiply(k, 0, yy, prof)
         return rotate_parts(total)
 
@@ -173,8 +174,14 @@
     trace_copies = [to_layer(k, my_trace, tr_send, traces, tr_recv) for k in range(3)]
     field_copies = [to_layer(k, my_field, mid_send, fields, mid_recv) for k in range(3)]
 
-    seg[0, y * Z + z, c] = forces[way_01]
+    force = find_force(0)
+    seg[0, y * Z + z, c] = force
+    pl.semaphore_wait(barrier, len(peers))
     send_own(0)
+    for copy in mat_copies:
+        copy.start()
+    forces[way_01] = force
+    forces[1 - way_01] = find_force(1)
     for copy in profile_copies:
         copy.start()
 
@@ -238,12 +245,20 @@
         mid_out[0, part] = moved[:, part * 256:(part + 1) * 256]
 
     for k in range(3):
-        wait_bytes(seg.at[k, pl.ds(0, 5)], w1_send.at[k])
-        wait_bytes(seg.at[k, pl.ds(0, 21), 0, pl.ds(0, 64 - PART)], b_send.at[k])
-        wait_bytes(seg.at[k, pl.ds(0, 21), 0, pl.ds(0, PART)], a_send.at[k])
-        wait_bytes(seg.at[k, :, 0], sib_send.at[k])
+        wait_bytes(seg.at[:, pl.ds(0, 21), 0], seg_send.at[k])
         trace_copies[k].wait_send()
         field_copies[k].wait_send()
+
+
+def store(down, up, mid, down_out, up_out, mid_out, sem):
+    copies = [
+        pltpu.make_async_copy(src, dst, sem.at[i])
+        for i, (src, dst) in enumerate(((mid, mid_out), (down, down_out), (up, up_out)))
+    ]
+    for copy in copies:
+        copy.start()
+    for copy in copies:
+        copy.wait()
 
 
 def body(
@@ -252,18 +267,19 @@
     hbm = pl.BlockSpec(memory_space=pl.ANY)
     vmem = pl.BlockSpec(memory_space=pltpu.VMEM)
     dma = pltpu.SemaphoreType.DMA
-    return pl.pallas_call(
+    outs = (
+        jax.ShapeDtypeStruct((1, 2, 64, 256), BF16),
+        jax.ShapeDtypeStruct((1, 2, 64, 256), BF16),
+        jax.ShapeDtypeStruct((1, 2, 64, 256), F32),
+    )
+    results = pl.pallas_call(
         kernel,
-        out_shape=(
-            jax.ShapeDtypeStruct((1, 2, 64, 256), BF16),
-            jax.ShapeDtypeStruct((1, 2, 64, 256), BF16),
-            jax.ShapeDtypeStruct((1, 2, 64, 256), F32),
-        ),
+        out_shape=outs,
         in_specs=[pl.BlockSpec(memory_space=pltpu.SMEM), vmem] + [hbm] * 6,
         out_specs=(vmem, vmem, vmem),
         scratch_shapes=[
             pltpu.VMEM((2, 2, 2, 2, 64, 4096), BF16),
-            pltpu.VMEM((2, 2, 2, 64, 4096), BF16),
+            *[pltpu.VMEM((2, 2, 64, HALF), BF16)] * 4,
             pltpu.VMEM((3, Y * Z, CORES, 64, 128), BF16),
             pltpu.VMEM((4, 64, 128), BF16),
             pltpu.VMEM((4, 64, 128), F32),
@@ -273,9 +289,9 @@
             pltpu.VMEM((512, 512), BF16),
             pltpu.VMEM((4, 8, 128), jnp.int32),
             pltpu.SMEM((4, 8, 128), jnp.int32),
-            dma((4,)), dma((2,)),
-            dma((3, 7)), dma((3, 3)), dma((3, 3)), dma((3, 3)), dma((3, 4)),
-            dma((3,)), dma((3,)), dma((3,)), dma((3,)),
+            pltpu.VMEM((4096, 128), BF16),
+            dma((4,)), dma((2, 2)),
+            dma((3,)), dma((3, Y * Z)), dma((3, Y)),
             dma((3,)), dma((4,)), dma((3,)), dma((4,)),
             dma((4,)), dma((4,)), dma(()),
         ],
@@ -288,6 +304,14 @@
         profile, source_depth.reshape(1, 256),
         transfer_down, transfer_up, field_from_top, field_from_bottom, source_to_bottom, source_to_top,
     )
+    return pl.pallas_call(
+        store,
+        out_shape=outs,
+        in_specs=[vmem] * 3,
+        out_specs=(hbm,) * 3,
+        scratch_shapes=[dma((3,))],
+        name="store",
+    )(*results)
 
 
 def solution(mesh):

time: 60.5 us -> 55.5 us (0.917)
  local copies, waits for them, and re-layouts: 4.51 us -> 0 us
    unnamed x3 -> x0, local copies, waits for them, and re-layouts: 4.51 us -> none
    pallas_call x1 -> x2, Pallas kernels: 54.5 us -> 54.1 us  [the longest x1 52.4 us: body(): pl.pallas_call(kernel, out_shape=outs, in_specs=[pl.BlockSpec(memory_spac...]
where the time goes in v2:
time: 55.5 us; the launch traced here: 55.4 us
  Pallas kernels  54.1 us (97%)
  between operations  1.29 us (2%)
    pallas_call x1, Pallas kernels, body(): pl.pallas_call(kernel, out_shape=outs, in_specs=[pl.BlockSpec(memory_spac...  52.4 us
    pallas_call x1, Pallas kernels, body(): pl.pallas_call(store, out_shape=outs, in_specs=[vmem] * 3, out_specs=(hbm...  1.7 us

profile of v2, /device:TPU:1, one launch (start us, length us, event | category | flops | bytes accessed | tf_op | source)
XLA Modules:
  0.0 55.4 jit_solution(16253763823535875870)
XLA Ops:
  1.3 52.4 %sweeps.1 = (bf16[1,2,64,256]{3,2,1,0:T(8,128)(2,1)}, bf16[1,2,64,256]{3,2,1,0:T(8,128)(2,1)}, f32[1,2,64,256]{3,2,1,0:T(8,128)}) custom-call(s32[1]{0:T(128)S(6)} %copy.11.profile, s32[1,256]{1,0:T(1,128)} %bitcast.1, bf16[2,2,64,4096]{3,2,1,0:T(8,128)(2,1)} %t_down.1, bf16[2,2,64,4096]{3,2,1,0:T(8,128)(2,1)} %t_up.1, bf16[2,2,64,4096]{3,2,1,0:T(8,128)(2,1)} %f_top.1, ...), custom_call_target="tpu_custom_call" | custom-call | flops 1000000000 | bytes 13631488 | tf_op jit(solution)/shard_map/sweeps/pallas_call | solution.py:275
  53.7 1.7 %store.1 = (bf16[1,2,64,256]{3,2,1,0:T(8,128)(2,1)}, bf16[1,2,64,256]{3,2,1,0:T(8,128)(2,1)}, f32[1,2,64,256]{3,2,1,0:T(8,128)}) custom-call(bf16[1,2,64,256]{3,2,1,0:T(8,128)(2,1)} %get-tuple-element.6.down, bf16[1,2,64,256]{3,2,1,0:T(8,128)(2,1)} %get-tuple-element.7.up, f32[1,2,64,256]{3,2,1,0:T(8,128)} %get-tuple-element.8.mid), custom_call_target="tpu_custom_call" | custom-call | tf_op jit(solution)/shard_map/store/pallas_call | solution.py:307

commit v3 on v2

--- a/solution.py
+++ b/solution.py
@@ -13,6 +13,8 @@
 FAR_FIRST.sort(key=lambda o: -abs(o[0]) - abs(o[1]))
 STRAIGHT = [o for o in FAR_FIRST if 0 in o]
 OFFSETS = sorted(FAR_FIRST, key=lambda o: abs(o[0]) + abs(o[1]) + (0 if 0 in o else 3.6))
+ORDER = [(0, 0)] + OFFSETS
+GROUPS = {26: (0, 20), 31: (20, 32)}
 CHUNK, HALF = 1024, 2048
 BF16, F32 = jnp.bfloat16, jnp.float32
 
@@ -32,7 +34,7 @@
     profile, depth, t_down, t_up, f_top, f_bottom, s_bottom, s_top,
     down_out, up_out, mid_out,
     mats, src_0, src_1, src_2, src_3, seg, traces, fields, forces, my_trace, my_field, place, prof_v, prof_s,
-    hot, mat_sem, src_sem, seg_send, seg_recv, sib_recv, tr_send, tr_recv, mid_send, mid_recv, p_send, p_recv, p_local,
+    hot, own_profile, depth_v, small_sem, mat_sem, src_sem, seg_send, seg_recv, sib_recv, tr_send, tr_recv, mid_send, mid_recv, p_send, p_recv, p_local,
 ):
     layers = 4
     srcs = (src_0, src_1, src_2, src_3)
@@ -67,14 +69,23 @@
             for copy in src_copies[way]:
                 copy.start()
     mat_copies = [
-        pltpu.make_async_copy(ref, mats.at[i // 2, i % 2], mat_sem.at[i])
-        for i, ref in enumerate((t_down, f_top, t_up, f_bottom))
+        pltpu.make_async_copy(
+            ref.at[:, :, :, pl.ds(pl.multiple_of((((y - dy) % Y) * Z + (z - dz) % Z) * 128, 128), 128)],
+            mats.at[i // 2, i % 2, :, :, :, pl.ds(place_in * 128, 128)],
+            mat_sem.at[i],
+        )
+        for i, ref in enumerate((t_down, f_top, t_up, f_bottom)) for place_in, (dy, dz) in enumerate(ORDER)
     ]
 
-    my_profile = profile[0]
+    copies = [pltpu.make_async_copy(profile, own_profile, small_sem.at[0]), pltpu.make_async_copy(depth, depth_v, small_sem.at[1])]
+    for copy in copies:
+        copy.start()
+    for copy in copies:
+        copy.wait()
+    my_profile = own_profile[0]
     prof_v[r] = jnp.full(prof_v.shape[1:], my_profile, jnp.int32)
 
-    every = depth[...]
+    every = depth_v[...]
     pick_s = lax.broadcasted_iota(jnp.int32, (256, 128), 0)
     pick_j = lax.broadcasted_iota(jnp.int32, (256, 128), 1)
     pick = jnp.where(pick_s == 4 * (pick_j % 64) + r, 1.0, 0.0).astype(BF16)
@@ -114,8 +125,11 @@
     def block(k, offset):
         return seg.at[k, ((y - offset[0]) % Y) * Z + (z - offset[1]) % Z, c]
 
-    def row(k, yy, core):
-        return seg.at[k, pl.ds((yy % Y) * Z, Z), core]
+    def sib_block(k, offset):
+        return seg.at[k, ((y - offset[0]) % Y) * Z + (z - offset[1]) % Z, 1 - c]
+
+    def index(offset):
+        return (offset[0] % Y) * Z + offset[1] % Z
 
     def put(ref, send, recv, to):
         pltpu.make_async_remote_copy(
@@ -124,12 +138,12 @@
 
     def ship(k, held, offset):
         put(
-            block(k, held), seg_send.at[k], seg_recv.at[k, (offset[0] % Y) * Z + offset[1] % Z],
+            block(k, held), seg_send.at[k], seg_recv.at[k, index(offset)],
             at(y + offset[0] - held[0], z + offset[1] - held[1], c),
         )
 
     def to_sibling(k, held):
-        put(block(k, held), seg_send.at[k], sib_recv.at[k, held[0] % Y], sibling)
+        put(block(k, held), seg_send.at[k], sib_recv.at[k, index(held)], sibling)
 
     def send_own(k):
         for offset in STRAIGHT:
@@ -137,33 +151,49 @@
         to_sibling(k, (0, 0))
 
     def pass_on(k, held):
-        wait_bytes(block(k, held), seg_recv.at[k, (held[0] % Y) * Z + held[1] % Z])
+        wait_bytes(block(k, held), seg_recv.at[k, index(held)])
         for offset in FAR_FIRST:
             if 0 not in offset:
                 if (offset[0], 0) == held if abs(offset[1]) <= 2 else (0, offset[1]) == held:
                     ship(k, held, offset)
         to_sibling(k, held)
 
-    def multiply(k, kind, yy, prof):
-        left = mats[ways[k], kind, prof, :, :, pl.ds(pl.multiple_of(yy * 1024, 1024), 1024)]
-        right = seg[k, pl.ds(yy * Z, Z)].reshape(1024, 128)
-        return jnp.dot(left.reshape(128, 1024), right, preferred_element_type=F32)
-
-    def collect(k, prof):
-        for held in OFFSETS:
+    def get_ready():
+        for i in range(4):
+            wait_bytes(mats.at[i // 2, i % 2], mat_sem.at[i])
+        for k in range(1, layers):
+            other = (r + k) % layers
+            wait_bytes(prof_v.at[other], p_recv.at[other])
+        for copy in profile_copies:
+            copy.wait_send()
+        to_scalar = pltpu.make_async_copy(prof_v, prof_s, p_local)
+        to_scalar.start()
+        to_scalar.wait()
+
+    def multiply(k, kind, group, prof):
+        first, end = group
+        left = mats[ways[k], kind, prof, :, :, pl.ds(first * 128, (end - first) * 128)]
+        right = [seg[k, ((y - dy) % Y) * Z + (z - dz) % Z].reshape(128, 128) for dy, dz in ORDER[first:end]]
+        return jnp.dot(left.reshape(128, -1), jnp.concatenate(right, axis=0), preferred_element_type=F32)
+
+    def collect(k):
+        kinds = (0, 1) if k == 2 else (0,)
+        totals = [jnp.zeros((128, 128), F32) for _ in kinds]
+        for n, held in enumerate(OFFSETS, 1):
             pass_on(k, held)
-        total = jnp.zeros((128, 128), F32)
-        for dy in (0, 1, -1, 2):
-            yy = (y - dy) % Y
-            wait_bytes(row(k, yy, 1 - c), sib_recv.at[k, dy % Y])
-            total += multiply(k, 0, yy, prof)
-        return rotate_parts(total)
-
-    def field(k, prof):
-        total = jnp.zeros((128, 128), F32)
-        for yy in range(Y):
-            total += multiply(k, 1, yy, prof)
-        return rotate_parts(total)
+            if n == len(STRAIGHT) and k == 0:
+                get_ready()
+            if n in GROUPS:
+                for offset in ORDER[slice(*GROUPS[n])]:
+                    wait_bytes(sib_block(k, offset), sib_recv.at[k, index(offset)])
+                prof = prof_s[layer_of[k], 0, 0]
+                for t, kind in enumerate(kinds):
+                    totals[t] += multiply(k, kind, GROUPS[n], prof)
+        return [rotate_parts(total) for total in totals]
+
+    def field(k):
+        prof = prof_s[layer_of[k], 0, 0]
+        return rotate_parts(sum(multiply(k, 1, group, prof) for group in GROUPS.values()))
 
     def to_layer(k, mine, send, theirs, recv):
         return pltpu.make_async_remote_copy(
@@ -191,20 +221,9 @@
     place[...] = jnp.where(i_out == goal, 1.0, 0.0).astype(BF16)
     fields[r] = jnp.zeros((64, 128), F32)
 
-    for copy in mat_copies:
-        copy.wait()
-    for k in range(1, layers):
-        other = (r + k) % layers
-        wait_bytes(prof_v.at[other], p_recv.at[other])
-    to_scalar = pltpu.make_async_copy(prof_v, prof_s, p_local)
-    for copy in profile_copies:
-        copy.wait_send()
-    to_scalar.start()
-    to_scalar.wait()
-
     for k in range(3):
-        prof = prof_s[layer_of[k], 0, 0]
-        trace = collect(k, prof).astype(BF16)
+        results = collect(k)
+        trace = results[0].astype(BF16)
         my_trace[k] = trace
         if k == 0:
             seg[1, y * Z + z, c] = trace
@@ -213,7 +232,7 @@
         if k < 2:
             send_own(k + 1)
         trace_copies[k].start()
-        my_field[k] = field(k, prof)
+        my_field[k] = results[1] if k == 2 else field(k)
         field_copies[k].start()
 
     for k in range(1, layers):
@@ -274,8 +293,8 @@
     )
     results = pl.pallas_call(
         kernel,
-        out_shape=outs,
-        in_specs=[pl.BlockSpec(memory_space=pltpu.SMEM), vmem] + [hbm] * 6,
+        out_shape=tuple(pltpu.VMEM(o.shape, o.dtype) for o in outs),
+        in_specs=[hbm] * 8,
         out_specs=(vmem, vmem, vmem),
         scratch_shapes=[
             pltpu.VMEM((2, 2, 2, 2, 64, 4096), BF16),
@@ -290,8 +309,9 @@
             pltpu.VMEM((4, 8, 128), jnp.int32),
             pltpu.SMEM((4, 8, 128), jnp.int32),
             pltpu.VMEM((4096, 128), BF16),
+            pltpu.SMEM((1,), jnp.int32), pltpu.VMEM((1, 256), jnp.int32), dma((2,)),
             dma((4,)), dma((2, 2)),
-            dma((3,)), dma((3, Y * Z)), dma((3, Y)),
+            dma((3,)), dma((3, Y * Z)), dma((3, Y * Z)),
             dma((3,)), dma((4,)), dma((3,)), dma((4,)),
             dma((4,)), dma((4,)), dma(()),
         ],
@@ -311,7 +331,7 @@
         out_specs=(hbm,) * 3,
         scratch_shapes=[dma((3,))],
         name="store",
-    )(*results)
+    )(*[pltpu.with_memory_space_constraint(x, pltpu.VMEM) for x in results])
 
 
 def solution(mesh):

time: 55.5 us -> 53.6 us (0.966)
  Pallas kernels: 54.1 us -> 52.2 us
    pallas_call x1, Pallas kernels: 1.7 us -> 0.72 us  [body(): pl.pallas_call(store, out_shape=outs, in_specs=[vmem] * 3, out_specs=(hbm...]
    pallas_call x1, Pallas kernels: 52.4 us -> 51.5 us  [body(): pl.pallas_call(kernel, out_shape=tuple((pltpu.VMEM(o.shape, o.dtype) for...]
where the time goes in v3:
time: 53.6 us; the launch traced here: 53.5 us
  Pallas kernels  52.2 us (97%)
  between operations  1.29 us (2%)
    pallas_call x1, Pallas kernels, body(): pl.pallas_call(kernel, out_shape=tuple((pltpu.VMEM(o.shape, o.dtype) for...  51.5 us

profile of v3, /device:TPU:1, one launch (start us, length us, event | category | flops | bytes accessed | tf_op | source)
XLA Modules:
  0.0 53.5 jit_solution(131824061604993946)
XLA Ops:
  1.3 51.5 %sweeps.1 = (bf16[1,2,64,256]{3,2,1,0:T(8,128)(2,1)S(1)}, bf16[1,2,64,256]{3,2,1,0:T(8,128)(2,1)S(1)}, f32[1,2,64,256]{3,2,1,0:T(8,128)S(1)}) custom-call(s32[1]{0:T(128)S(6)} %copy.11.profile, s32[1,256]{1,0:T(1,128)} %bitcast.1, bf16[2,2,64,4096]{3,2,1,0:T(8,128)(2,1)} %t_down.1, bf16[2,2,64,4096]{3,2,1,0:T(8,128)(2,1)} %t_up.1, ...), custom_call_target="tpu_custom_call" | custom-call | flops 1000000000 | bytes 13631488 | tf_op jit(solution)/shard_map/sweeps/pallas_call | solution.py:294
  52.8 0.7 %store.1 = (bf16[1,2,64,256]{3,2,1,0:T(8,128)(2,1)}, bf16[1,2,64,256]{3,2,1,0:T(8,128)(2,1)}, f32[1,2,64,256]{3,2,1,0:T(8,128)}) custom-call(bf16[1,2,64,256]{3,2,1,0:T(8,128)(2,1)S(1)} %get-tuple-element.6.down, bf16[1,2,64,256]{3,2,1,0:T(8,128)(2,1)S(1)} %get-tuple-element.7.up, f32[1,2,64,256]{3,2,1,0:T(8,128)S(1)} %get-tuple-element.8.mid), custom_call_target="tpu_custom_call" | custom-call | tf_op jit(solution)/shard_map/store/pallas_call | solution.py:327

commit v4 on v3

--- a/solution.py
+++ b/solution.py
@@ -12,7 +12,10 @@
 FAR_FIRST = [(dy, dz) for dy in (0, 1, -1, 2) for dz in (0, 1, -1, 2, -2, 3, -3, 4) if (dy, dz) != (0, 0)]
 FAR_FIRST.sort(key=lambda o: -abs(o[0]) - abs(o[1]))
 STRAIGHT = [o for o in FAR_FIRST if 0 in o]
-OFFSETS = sorted(FAR_FIRST, key=lambda o: abs(o[0]) + abs(o[1]) + (0 if 0 in o else 3.6))
+OFFSETS = sorted(
+    FAR_FIRST,
+    key=lambda o: (0 not in o or 0 < abs(o[1]) <= 2, 0 not in o, o[1] != 0 and 0 in o, abs(o[0]) + abs(o[1])),
+)
 ORDER = [(0, 0)] + OFFSETS
 GROUPS = {26: (0, 20), 31: (20, 32)}
 CHUNK, HALF = 1024, 2048
@@ -34,7 +37,7 @@
     profile, depth, t_down, t_up, f_top, f_bottom, s_bottom, s_top,
     down_out, up_out, mid_out,
     mats, src_0, src_1, src_2, src_3, seg, traces, fields, forces, my_trace, my_field, place, prof_v, prof_s,
-    hot, own_profile, depth_v, small_sem, mat_sem, src_sem, seg_send, seg_recv, sib_recv, tr_send, tr_recv, mid_send, mid_recv, p_send, p_recv, p_local,
+    hot, own_profile, depth_v, small_sem, mat_sem, src_sem, seg_send, seg_recv, sib_recv, tr_send, tr_recv, mid_send, mid_recv, p_send, p_recv, p_local, x_send,
 ):
     layers = 4
     srcs = (src_0, src_1, src_2, src_3)
@@ -110,9 +113,9 @@
         return jnp.where(lane < 64, total[:64], total[64:]).astype(BF16)
 
     middle = jnp.logical_or(r == 1, r == 2)
-    way_2 = jnp.where(r % 2 == 0, 0, 1)
-    ways = (way_01, way_01, way_2)
-    layer_of = (jnp.where(r % 2 == 0, 1, 2), jnp.where(r < 2, r + 2, r - 2), jnp.where(r % 2 == 0, 3, 0))
+    outer = jnp.logical_not(middle)
+    ways = (way_01, r % 2, 1 - r % 2)
+    layer_of = (1 + r % 2, jnp.where(r == 0, 2, jnp.where(r == 1, 0, jnp.where(r == 2, 3, 1))), 3 * (r % 2))
 
     profile_copies = [
         pltpu.make_async_remote_copy(
@@ -145,10 +148,13 @@
     def to_sibling(k, held):
         put(block(k, held), seg_send.at[k], sib_recv.at[k, index(held)], sibling)
 
-    def send_own(k):
-        for offset in STRAIGHT:
-            ship(k, (0, 0), offset)
-        to_sibling(k, (0, 0))
+    def send_own(k, src, plane):
+        own = block(k, (0, 0))
+        for dy, dz in STRAIGHT:
+            pltpu.make_async_remote_copy(
+                src_ref=src, dst_ref=own, send_sem=seg_send.at[k], recv_sem=seg_recv.at[k, index((dy, dz))],
+                device_id=(plane, ((y + dy) % Y * Z + (z + dz) % Z) * CORES + c), device_id_type=MESH,
+            ).start()
 
     def pass_on(k, held):
         wait_bytes(block(k, held), seg_recv.at[k, index(held)])
@@ -179,6 +185,11 @@
     def collect(k):
         kinds = (0, 1) if k == 2 else (0,)
         totals = [jnp.zeros((128, 128), F32) for _ in kinds]
+        if k == 2:
+            @pl.when(outer)
+            def _():
+                wait_bytes(block(2, (0, 0)), seg_recv.at[2, 0])
+                to_sibling(2, (0, 0))
         for n, held in enumerate(OFFSETS, 1):
             pass_on(k, held)
             if n == len(STRAIGHT) and k == 0:
@@ -207,7 +218,8 @@
     force = find_force(0)
     seg[0, y * Z + z, c] = force
     pl.semaphore_wait(barrier, len(peers))
-    send_own(0)
+    send_own(0, block(0, (0, 0)), r)
+    to_sibling(0, (0, 0))
     for copy in mat_copies:
         copy.start()
     forces[way_01] = force
@@ -221,23 +233,55 @@
     place[...] = jnp.where(i_out == goal, 1.0, 0.0).astype(BF16)
     fields[r] = jnp.zeros((64, 128), F32)
 
+    across = pltpu.make_async_remote_copy(
+        src_ref=my_trace.at[1], dst_ref=block(2, (0, 0)), send_sem=x_send, recv_sem=seg_recv.at[2, 0],
+        device_id=(3 - r, d), device_id_type=MESH,
+    )
+
     for k in range(3):
         results = collect(k)
         trace = results[0].astype(BF16)
-        my_trace[k] = trace
+        if k < 2:
+            my_trace[k] = trace
         if k == 0:
-            seg[1, y * Z + z, c] = trace
+            seg[1, y * Z + z, c] = jnp.where(middle, forces[1 - way_01], trace)
+            send_own(1, block(1, (0, 0)), r)
+            to_sibling(1, (0, 0))
+
+            @pl.when(middle)
+            def _():
+                seg[2, y * Z + z, c] = trace
+                send_own(2, block(2, (0, 0)), r)
+                to_sibling(2, (0, 0))
         elif k == 1:
-            seg[2, y * Z + z, c] = jnp.where(middle, forces[1 - way_01], trace)
+            @pl.when(outer)
+            def _():
+                send_own(2, my_trace.at[1], 3 - r)
+                across.start()
         if k < 2:
-            send_own(k + 1)
-        trace_copies[k].start()
-        my_field[k] = results[1] if k == 2 else field(k)
-        field_copies[k].start()
+            trace_copies[k].start()
+            my_field[k] = field(k)
+            field_copies[k].start()
+
+    @pl.when(middle)
+    def _():
+        my_trace[2] = trace
+        my_field[2] = results[1]
+        trace_copies[2].start()
+        field_copies[2].start()
+
+    @pl.when(outer)
+    def _():
+        traces[3 - r] = trace
+        fields[3 - r] = results[1]
 
     for k in range(1, layers):
         other = (r + k) % layers
-        wait_bytes(traces.at[other], tr_recv.at[other])
+
+        @pl.when(jnp.logical_or(middle, other != 3 - r))
+        def _():
+            wait_bytes(traces.at[other], tr_recv.at[other])
+            wait_bytes(fields.at[other], mid_recv.at[other])
     traces[r] = forces[0]
     empty = jnp.zeros((64, 128), BF16)
     down = [jnp.where(i <= r, traces[i], empty) for i in range(layers)]
@@ -249,9 +293,6 @@
         down_out[0, part] = moved[:64, part * 256:(part + 1) * 256]
         up_out[0, part] = moved[64:, part * 256:(part + 1) * 256]
 
-    for k in range(1, layers):
-        other = (r + k) % layers
-        wait_bytes(fields.at[other], mid_recv.at[other])
     whole = jnp.concatenate([fields[i] for i in range(layers)], axis=1)
     first = whole.astype(BF16)
     rest = whole - first.astype(F32)
@@ -265,8 +306,18 @@
 
     for k in range(3):
         wait_bytes(seg.at[:, pl.ds(0, 21), 0], seg_send.at[k])
+    for k in range(2):
         trace_copies[k].wait_send()
         field_copies[k].wait_send()
+
+    @pl.when(middle)
+    def _():
+        trace_copies[2].wait_send()
+        field_copies[2].wait_send()
+
+    @pl.when(outer)
+    def _():
+        across.wait_send()
 
 
 def store(down, up, mid, down_out, up_out, mid_out, sem):
@@ -314,6 +365,7 @@
             dma((3,)), dma((3, Y * Z)), dma((3, Y * Z)),
             dma((3,)), dma((4,)), dma((3,)), dma((4,)),
             dma((4,)), dma((4,)), dma(()),
+            dma(()),
         ],
         compiler_params=pltpu.CompilerParams(
             collective_id=0, has_side_effects=True, vmem_limit_bytes=60 * 2**20

time: 53.6 us -> 51.3 us (0.957)
  Pallas kernels: 52.2 us -> 50 us
    pallas_call x1, Pallas kernels: 51.5 us -> 49.2 us  [body(): pl.pallas_call(kernel, out_shape=tuple((pltpu.VMEM(o.shape, o.dtype) for...]
where the time goes in v4:
time: 51.3 us; the launch traced here: 51.2 us
  Pallas kernels  50 us (97%)
  between operations  1.29 us (3%)
    pallas_call x1, Pallas kernels, body(): pl.pallas_call(kernel, out_shape=tuple((pltpu.VMEM(o.shape, o.dtype) for...  49.2 us

profile of v4, /device:TPU:1, one launch (start us, length us, event | category | flops | bytes accessed | tf_op | source)
XLA Modules:
  0.0 51.2 jit_solution(9594680465900188277)
XLA Ops:
  1.3 49.2 %sweeps.1 = (bf16[1,2,64,256]{3,2,1,0:T(8,128)(2,1)S(1)}, bf16[1,2,64,256]{3,2,1,0:T(8,128)(2,1)S(1)}, f32[1,2,64,256]{3,2,1,0:T(8,128)S(1)}) custom-call(s32[1]{0:T(128)S(6)} %copy.11.profile, s32[1,256]{1,0:T(1,128)} %bitcast.1, bf16[2,2,64,4096]{3,2,1,0:T(8,128)(2,1)} %t_down.1, bf16[2,2,64,4096]{3,2,1,0:T(8,128)(2,1)} %t_up.1, ...), custom_call_target="tpu_custom_call" | custom-call | flops 1000000000 | bytes 13631488 | tf_op jit(solution)/shard_map/sweeps/pallas_call | solution.py:345
  50.5 0.7 %store.1 = (bf16[1,2,64,256]{3,2,1,0:T(8,128)(2,1)}, bf16[1,2,64,256]{3,2,1,0:T(8,128)(2,1)}, f32[1,2,64,256]{3,2,1,0:T(8,128)}) custom-call(bf16[1,2,64,256]{3,2,1,0:T(8,128)(2,1)S(1)} %get-tuple-element.6.down, bf16[1,2,64,256]{3,2,1,0:T(8,128)(2,1)S(1)} %get-tuple-element.7.up, f32[1,2,64,256]{3,2,1,0:T(8,128)S(1)} %get-tuple-element.8.mid), custom_call_target="tpu_custom_call" | custom-call | tf_op jit(solution)/shard_map/store/pallas_call | solution.py:379

commit v5 on v4

--- a/solution.py
+++ b/solution.py
@@ -11,7 +11,7 @@
 Y, Z, CORES = 4, 8, 2
 FAR_FIRST = [(dy, dz) for dy in (0, 1, -1, 2) for dz in (0, 1, -1, 2, -2, 3, -3, 4) if (dy, dz) != (0, 0)]
 FAR_FIRST.sort(key=lambda o: -abs(o[0]) - abs(o[1]))
-STRAIGHT = [o for o in FAR_FIRST if 0 in o]
+STRAIGHT = [o for o in FAR_FIRST if 0 in o or abs(o[0]) == abs(o[1]) == 1]
 OFFSETS = sorted(
     FAR_FIRST,
     key=lambda o: (0 not in o or 0 < abs(o[1]) <= 2, 0 not in o, o[1] != 0 and 0 in o, abs(o[0]) + abs(o[1])),
@@ -52,6 +52,7 @@
 
     barrier = pltpu.get_barrier_semaphore()
     peers = [at(y, z + k, c) for k in range(1, Z)] + [at(y + k, z, c) for k in range(1, Y)] + [sibling]
+    peers += [at(y + i, z + j, c) for i in (1, -1) for j in (1, -1)]
     peers += [((r + k) % layers, d) for k in range(1, layers)]
     for peer in peers:
         pl.semaphore_signal(barrier, inc=1, device_id=peer, device_id_type=MESH)
@@ -159,7 +160,7 @@
     def pass_on(k, held):
         wait_bytes(block(k, held), seg_recv.at[k, index(held)])
         for offset in FAR_FIRST:
-            if 0 not in offset:
+            if offset not in STRAIGHT:
                 if (offset[0], 0) == held if abs(offset[1]) <= 2 else (0, offset[1]) == held:
                     ship(k, held, offset)
         to_sibling(k, held)
@@ -345,7 +346,7 @@
     results = pl.pallas_call(
         kernel,
         out_shape=tuple(pltpu.VMEM(o.shape, o.dtype) for o in outs),
-        in_specs=[hbm] * 8,
+        in_specs=[vmem] + [hbm] * 7,
         out_specs=(vmem, vmem, vmem),
         scratch_shapes=[
             pltpu.VMEM((2, 2, 2, 2, 64, 4096), BF16),

time: 51.3 us -> 53.2 us (1.037)
  Pallas kernels: 50 us -> 51.8 us
    pallas_call x1, Pallas kernels: 49.2 us -> 51 us  [body(): pl.pallas_call(kernel, out_shape=tuple((pltpu.VMEM(o.shape, o.dtype) for...]
where the time goes in v5:
time: 53.2 us; the launch traced here: 53.1 us
  Pallas kernels  51.8 us (97%)
  between operations  1.29 us (2%)
    pallas_call x1, Pallas kernels, body(): pl.pallas_call(kernel, out_shape=tuple((pltpu.VMEM(o.shape, o.dtype) for...  51 us

profile of v5, /device:TPU:1, one launch (start us, length us, event | category | flops | bytes accessed | tf_op | source)
XLA Modules:
  0.0 53.1 jit_solution(643956484403474650)
XLA Ops:
  1.3 51.0 %sweeps.1 = (bf16[1,2,64,256]{3,2,1,0:T(8,128)(2,1)S(1)}, bf16[1,2,64,256]{3,2,1,0:T(8,128)(2,1)S(1)}, f32[1,2,64,256]{3,2,1,0:T(8,128)S(1)}) custom-call(s32[1]{0:T(128)S(6)} %copy.11.profile, s32[1,256]{1,0:T(1,128)} %bitcast.1, bf16[2,2,64,4096]{3,2,1,0:T(8,128)(2,1)} %t_down.1, bf16[2,2,64,4096]{3,2,1,0:T(8,128)(2,1)} %t_up.1, ...), custom_call_target="tpu_custom_call" | custom-call | flops 1000000000 | bytes 13631488 | tf_op jit(solution)/shard_map/sweeps/pallas_call | solution.py:346
  52.3 0.7 %store.1 = (bf16[1,2,64,256]{3,2,1,0:T(8,128)(2,1)}, bf16[1,2,64,256]{3,2,1,0:T(8,128)(2,1)}, f32[1,2,64,256]{3,2,1,0:T(8,128)}) custom-call(bf16[1,2,64,256]{3,2,1,0:T(8,128)(2,1)S(1)} %get-tuple-element.6.down, bf16[1,2,64,256]{3,2,1,0:T(8,128)(2,1)S(1)} %get-tuple-element.7.up, f32[1,2,64,256]{3,2,1,0:T(8,128)S(1)} %get-tuple-element.8.mid), custom_call_target="tpu_custom_call" | custom-call | tf_op jit(solution)/shard_map/store/pallas_call | solution.py:380
